TPU v7x, 512 devices: a whole 4x4x16 slice. The times are simulated.
512 devices in a mesh: dp: 32 (over y, z_lo), seq: 16 (over x, z_hi, core).
Axes of the slice: x: 4, y: 4, z: 16 (z_hi: 2, z_lo: 8; z = z_hi * 8 + z_lo), core: 2. Of those that a mesh axis runs over, the one named last changes fastest.
Arguments:
- q_in: bfloat16 [65536, 4096], P(('dp', 'seq')), may hold values from -200 to 200
- k_in: bfloat16 [65536, 4096], P(('dp', 'seq')), may hold values from -200 to 200
- v_in: bfloat16 [65536, 4096], P(('dp', 'seq')), may hold values from -6 to 6
- cotangent: bfloat16 [65536, 4096], P(('dp', 'seq')), may hold values from -6 to 6
- owner: int32 [32, 16], P('dp'), may hold values from 0 to 15, each once within a row
- gain_q: float32 [4096], P('seq'), may hold values from 0.1 to 1.9
- gain_k: float32 [4096], P('seq'), may hold values from 0.1 to 1.9
Outputs:
- grad_gain_q: float32 [4096], P(('seq', 'dp'))
- grad_gain_k: float32 [4096], P(('seq', 'dp'))
Inputs may be any that keep to these rules, and one draw needn't show every extreme that they name: `owner`: each row is a permutation; slot s belongs to clip s // 8, time span s % 8 of it.
All inputs are finite; a program needn't handle non-finite values.
Results may differ from a plain program's by a relative error of at most 0.03.
Values may be sent and summed in bfloat16 or wider, within the bound.
A program may use at most 64 MiB of HBM per device.

v0:
```python
import jax
import jax.numpy as jnp
from jax import lax
from jax.sharding import PartitionSpec as P

HEADS = 32
HEAD_DIM = 128
CLIPS_GRP = 2
HD_ALL = 4096


EPSILON = 1e-06


def rope_tables(positions, head_depth):
    half_depth = head_depth // 2
    frequency = 10000.0 ** (-jnp.arange(half_depth, dtype=jnp.float32) / half_depth)
    angles = positions.astype(jnp.float32)[:, None] * frequency[None, :]
    return (jnp.cos(angles)[:, None, :], jnp.sin(angles)[:, None, :])


def rotate(field, cosine_table, sine_table):
    half_depth = field.shape[-1] // 2
    first_half = field[..., :half_depth]
    second_half = field[..., half_depth:]
    return jnp.concatenate(
        [
            first_half * cosine_table - second_half * sine_table,
            first_half * sine_table + second_half * cosine_table,
        ],
        axis=-1,
    )


def unrotate(field, cosine_table, sine_table):
    half_depth = field.shape[-1] // 2
    first_half = field[..., :half_depth]
    second_half = field[..., half_depth:]
    return jnp.concatenate(
        [
            first_half * cosine_table + second_half * sine_table,
            second_half * cosine_table - first_half * sine_table,
        ],
        axis=-1,
    )


def clip_grads(pieces):
    queries, key_rows, values, upstream = pieces
    factor = queries.shape[-1] ** (-0.5)
    scores = jnp.dot(queries, key_rows.T, preferred_element_type=jnp.float32) * factor
    row_max = jnp.max(scores, axis=1, keepdims=True)
    lifted = jnp.exp(scores - row_max)
    weights = lifted / jnp.sum(lifted, axis=1, keepdims=True)
    slopes = jnp.dot(upstream, values.T, preferred_element_type=jnp.float32)
    center = jnp.sum(weights * slopes, axis=1, keepdims=True)
    dscore = (weights * (slopes - center)).astype(jnp.bfloat16)
    dquery = (jnp.dot(dscore, key_rows, preferred_element_type=jnp.float32) * factor).astype(
        jnp.bfloat16
    )
    dkey_rows = (jnp.dot(dscore.T, queries, preferred_element_type=jnp.float32) * factor).astype(
        jnp.bfloat16
    )
    return (dquery, dkey_rows)


def head_items(field, clip_count):
    row_count, head_count, head_depth = field.shape
    clip_rows = row_count // clip_count
    return (
        field.reshape(clip_count, clip_rows, head_count, head_depth)
        .transpose(2, 0, 1, 3)
        .reshape(head_count * clip_count, clip_rows, head_depth)
    )


def row_items(field, clip_count, head_count):
    item_count, clip_rows, head_depth = field.shape
    return (
        field.reshape(head_count, clip_count, clip_rows, head_depth)
        .transpose(1, 2, 0, 3)
        .reshape(clip_count * clip_rows, head_count, head_depth)
    )


def attend(q_rot, k_rot, values, upstream, clip_count):
    head_count = q_rot.shape[1]
    pieces = tuple((head_items(field, clip_count) for field in (q_rot, k_rot, values, upstream)))
    dquery, dkey_rows = lax.map(clip_grads, pieces)
    return (row_items(dquery, clip_count, head_count), row_items(dkey_rows, clip_count, head_count))


def normalize(raw):
    widened = raw.astype(jnp.float32)
    return widened / jnp.sqrt(jnp.mean(widened * widened, axis=1, keepdims=True) + EPSILON)


def on_device(q_in, k_in, v_in, cotangent, owner, gain_q, gain_k):
    seq_count = lax.axis_size("seq")
    span_rows = q_in.shape[0]
    local_width = gain_q.shape[0]
    local_heads = local_width // HEAD_DIM
    group_rows = span_rows * seq_count
    chart = owner[0]
    slots = jnp.arange(seq_count, dtype=jnp.int32)
    holder = jnp.sum(jnp.where(chart[None, :] == slots[:, None], slots[None, :], 0), axis=1)
    head_shape = (group_rows, local_heads, HEAD_DIM)

    def by_slot(field):
        return jnp.take(field.reshape(seq_count, span_rows, local_width), holder, axis=0).reshape(
            group_rows, local_width
        )

    gains = (
        lax.all_gather(gain_q, "seq", axis=0, tiled=True),
        lax.all_gather(gain_k, "seq", axis=0, tiled=True),
    )
    slot = chart[lax.axis_index("seq")]
    spans_per_clip = seq_count // CLIPS_GRP
    own_positions = slot % spans_per_clip * span_rows + jnp.arange(span_rows, dtype=jnp.int32)
    cosine_table, sine_table = rope_tables(own_positions, HEAD_DIM)
    q_hat = normalize(q_in).reshape(span_rows, HEADS, HEAD_DIM)
    k_hat = normalize(k_in).reshape(span_rows, HEADS, HEAD_DIM)
    q_rot = (
        rotate(q_hat * gains[0].reshape(HEADS, HEAD_DIM), cosine_table, sine_table)
        .astype(jnp.bfloat16)
        .reshape(span_rows, HD_ALL)
    )
    k_rot = (
        rotate(k_hat * gains[1].reshape(HEADS, HEAD_DIM), cosine_table, sine_table)
        .astype(jnp.bfloat16)
        .reshape(span_rows, HD_ALL)
    )
    q_got, k_got, v_got, c_got = (
        lax.all_to_all(q_rot, "seq", split_axis=1, concat_axis=0, tiled=True),
        lax.all_to_all(k_rot, "seq", split_axis=1, concat_axis=0, tiled=True),
        lax.all_to_all(v_in, "seq", split_axis=1, concat_axis=0, tiled=True),
        lax.all_to_all(cotangent, "seq", split_axis=1, concat_axis=0, tiled=True),
    )
    dquery, dkey_rows = attend(
        by_slot(q_got).reshape(head_shape),
        by_slot(k_got).reshape(head_shape),
        by_slot(v_got).reshape(head_shape),
        by_slot(c_got).reshape(head_shape),
        CLIPS_GRP,
    )

    def by_device(field):
        return jnp.take(field.reshape(seq_count, span_rows, local_width), chart, axis=0).reshape(
            group_rows, local_width
        )

    dq_back, dk_back = (
        lax.all_to_all(
            by_device(dquery.reshape(group_rows, local_width)),
            "seq",
            split_axis=0,
            concat_axis=1,
            tiled=True,
        ),
        lax.all_to_all(
            by_device(dkey_rows.reshape(group_rows, local_width)),
            "seq",
            split_axis=0,
            concat_axis=1,
            tiled=True,
        ),
    )
    d_qn = unrotate(
        dq_back.astype(jnp.float32).reshape(span_rows, HEADS, HEAD_DIM), cosine_table, sine_table
    )
    d_kn = unrotate(
        dk_back.astype(jnp.float32).reshape(span_rows, HEADS, HEAD_DIM), cosine_table, sine_table
    )
    partial_grads = jnp.stack(
        [
            jnp.sum(d_qn * q_hat, axis=0).reshape(HD_ALL),
            jnp.sum(d_kn * k_hat, axis=0).reshape(HD_ALL),
        ]
    )
    head_sums = lax.psum_scatter(partial_grads, "seq", scatter_dimension=1, tiled=True)
    summed = lax.psum_scatter(head_sums, "dp", scatter_dimension=1, tiled=True)
    return (summed[0], summed[1])


def solution(mesh):
    return jax.shard_map(
        on_device,
        mesh=mesh,
        in_specs=(
            P(("dp", "seq"), None),
            P(("dp", "seq"), None),
            P(("dp", "seq"), None),
            P(("dp", "seq"), None),
            P("dp", None),
            P("seq"),
            P("seq"),
        ),
        out_specs=(P(("seq", "dp")), P(("seq", "dp"))),
        check_vma=False,
    )
```

profile of v0, /device:TPU:2, one launch (start us, length us, event | category | flops | bytes accessed | tf_op | source)
XLA Modules:
  0.0 743.1 jit_solution(3770012048922659314)
XLA Ops:
  10.4 1.5 fusion.27
  11.9 2.8 convert_divide_fusion
  14.8 2.0 copy.50
  16.8 47.2 %all-gather.1 = f32[16,1,256]{2,1,0:T(1,128)S(1)} all-gather(f32[1,1,256]{2,1,0:T(1,128)S(1)} %bitcast.136), channel_id=1, replica_groups=mesh['dp'=32,'seq'=16] {'seq'}, dimensions={0}, use_global_device_ids=true | all-gather | bytes 17408 | tf_op jit(solution)/shard_map/all_gather | solution.py:116
  64.3 1.6 convert_divide_fusion.1
  65.9 2.9 copy.47
  68.8 33.7 %all-gather = f32[16,1,256]{2,1,0:T(1,128)S(1)} all-gather(f32[1,1,256]{2,1,0:T(1,128)S(1)} %bitcast.137), channel_id=1, replica_groups=mesh['dp'=32,'seq'=16] {'seq'}, dimensions={0}, use_global_device_ids=true | all-gather | bytes 17408 | tf_op jit(solution)/shard_map/all_gather | solution.py:115
  105.7 1.3 copy.48
  107.0 14.4 %all-to-all-start = ((bf16[128,16,256]{2,0,1:T(8,128)(2,1)}), bf16[128,16,256]{2,0,1:T(8,128)(2,1)S(1)}, u32[]{:S(2)}, u32[]{:S(2)}) async-start(bf16[128,16,256]{2,0,1:T(8,128)(2,1)} %copy.48), calls=%async_computation | async-start | bytes 2097152 | tf_op jit(solution)/shard_map/all_to_all | solution.py:135
  121.4 1.3 copy.51
  122.7 26.1 %all-to-all-done = bf16[128,16,256]{2,0,1:T(8,128)(2,1)S(1)} async-done(((bf16[128,16,256]{2,0,1:T(8,128)(2,1)}), bf16[128,16,256]{2,0,1:T(8,128)(2,1)S(1)}, u32[]{:S(2)}, u32[]{:S(2)}) %all-to-all-start) | async-done | bytes 1048608 | tf_op jit(solution)/shard_map/all_to_all | solution.py:135
  148.9 6.6 all-to-all-start.1
  155.5 2.3 copy.53
  157.8 2.3 copy.54
  160.0 25.3 %all-to-all-done.1 = bf16[128,16,256]{2,0,1:T(8,128)(2,1)S(1)} async-done(((bf16[128,16,256]{2,0,1:T(8,128)(2,1)}), bf16[128,16,256]{2,0,1:T(8,128)(2,1)S(1)}, u32[]{:S(2)}, u32[]{:S(2)}) %all-to-all-start.1) | async-done | bytes 1048608 | tf_op jit(solution)/shard_map/all_to_all | solution.py:136
  185.3 14.6 %all-to-all-start.2 = ((bf16[128,16,256]{2,0,1:T(8,128)(2,1)}), bf16[128,16,256]{2,0,1:T(8,128)(2,1)}, u32[]{:S(2)}, u32[]{:S(2)}) async-start(bf16[128,16,256]{2,0,1:T(8,128)(2,1)} %copy.54), calls=%async_computation.2 | async-start | bytes 2097152 | tf_op jit(solution)/shard_map/all_to_all | solution.py:138
  199.9 2.3 copy.56
  202.2 2.3 copy.57
  204.5 36.6 %all-to-all-done.2 = bf16[128,16,256]{2,0,1:T(8,128)(2,1)} async-done(((bf16[128,16,256]{2,0,1:T(8,128)(2,1)}), bf16[128,16,256]{2,0,1:T(8,128)(2,1)}, u32[]{:S(2)}, u32[]{:S(2)}) %all-to-all-start.2) | async-done | bytes 1048608 | tf_op jit(solution)/shard_map/all_to_all | solution.py:138
  241.1 5.7 all-to-all-start.3
  247.6 1.8 gather_fusion.1
  249.5 2.8 gather_fusion.2
  252.3 33.7 %all-to-all-done.3 = bf16[128,16,256]{2,0,1:T(8,128)(2,1)} async-done(((bf16[128,16,256]{2,0,1:T(8,128)(2,1)}), bf16[128,16,256]{2,0,1:T(8,128)(2,1)}, u32[]{:S(2)}, u32[]{:S(2)}) %all-to-all-start.3) | async-done | bytes 1048608 | tf_op jit(solution)/shard_map/all_to_all | solution.py:137
  286.0 2.8 gather_fusion.3
  288.8 3.6 broadcast_select_fusion.2
  292.4 2.3 reshape_reshape_reshape.18
  294.7 1.4 copy.49
  297.2 1.4 copy.52
  298.6 2.1 reshape_reshape_reshape.20
  300.7 2.4 copy.55
  303.1 2.1 reshape_reshape_reshape.21
  305.2 2.3 copy.58
  307.6 30.6 %while.12 = (s32[]{:T(128)}, bf16[4,1024,128]{2,1,0:T(8,128)(2,1)}, bf16[4,1024,128]{2,1,0:T(8,128)(2,1)}, bf16[4,1024,128]{2,1,0:T(8,128)(2,1)S(1)}, bf16[4,102...) while((s32[]{:T(128)}, bf16[4,1024,128]{2,1,0:T(8,128)(2,1)}, ...), condition=%wide.region_7.9_spmd, body=%wide.region_3.0_spmd.sunk | while | flops 1091040256 | bytes 33595476 | solution.py:89
  309.0 2.1 multiply_reduce_fusion.7
  312.3 1.4 fusion.43
  313.7 1.5 fusion.42
  316.6 2.1 multiply_reduce_fusion.7
  320.0 1.4 fusion.43
  321.4 1.5 fusion.42
  324.3 2.1 multiply_reduce_fusion.7
  327.6 1.4 fusion.43
  329.1 1.5 fusion.42
  332.0 2.1 multiply_reduce_fusion.7
  335.3 1.4 fusion.43
  336.7 1.5 fusion.42
  338.2 2.3 copy.72
  341.2 2.3 copy.71
  343.5 1.5 reshape_reshape_reshape.23
  345.6 1.8 gather_fusion.5
  348.7 43.8 %all_to_all.78 = bf16[16,128,256]{2,1,0:T(8,128)(2,1)} all-to-all(bf16[16,128,256]{2,1,0:T(8,128)(2,1)S(1)} %get-tuple-element.77), channel_id=1, replica_groups=mesh['dp'=32,'seq'=16] {'seq'}, dimensions={0} | all-to-all | bytes 2097152 | tf_op jit(solution)/shard_map/all_to_all | solution.py:154
  392.5 4.2 all-to-all-start.5
  397.0 1.4 convert_bitcast_fusion.1
  398.5 1.9 copy.60
  400.3 30.6 %all-to-all-done.5 = bf16[16,128,256]{2,1,0:T(8,128)(2,1)} async-done(((bf16[16,128,256]{2,1,0:T(8,128)(2,1)}), bf16[16,128,256]{2,1,0:T(8,128)(2,1)}, u32[]{:S(2)}, u32[]{:S(2)}) %all-to-all-start.5) | async-done | bytes 1048608 | tf_op jit(solution)/shard_map/all_to_all | solution.py:161
  430.9 1.4 convert_bitcast_fusion
  432.4 1.8 copy.63
  434.2 4.2 multiply_add_fusion.1
  438.7 1.8 copy.61
  440.5 2.1 multiply_reduce_fusion.3
  442.8 1.8 copy.64
  444.7 2.0 multiply_reduce_fusion.2
  446.7 2.0 copy.65
  450.6 169.3 %reduce-scatter.5.cloned.1.call-done = f32[256,2]{1,0:T(8,128)} async-done(((f32[4096,2]{1,0:T(8,128)}), f32[256,2]{1,0:T(8,128)}) %reduce-scatter.5.cloned.1.call-update) | async-done | bytes 2064
  620.9 114.7 %all-reduce = f32[2,256]{1,0:T(2,128)S(1)} all-reduce(f32[2,256]{1,0:T(2,128)S(1)} %copy.66), channel_id=3, replica_groups=mesh['dp'=32,'seq'=16] {'dp'}, use_global_device_ids=true, to_apply=%region_11.13.clone | all-reduce | flops 512 | bytes 4096
  (66 shorter events, 23.3 us)
Async XLA Ops:
  14.8 2.0 copy-start.7
  14.8 49.3 %copy-start = (bf16[128,4096]{1,0:T(8,128)(2,1)S(1)}, bf16[128,4096]{1,0:T(8,128)(2,1)}, u32[]{:S(2)}) copy-start(bf16[128,4096]{1,0:T(8,128)(2,1)} %param.11) | copy-start | bytes 3145732
  65.9 2.9 copy-start.8
  102.7 1.6 copy-start.2
  107.0 41.8 %all-to-all-start = ((bf16[128,16,256]{2,0,1:T(8,128)(2,1)}), bf16[128,16,256]{2,0,1:T(8,128)(2,1)S(1)}, u32[]{:S(2)}, u32[]{:S(2)}) async-start(bf16[128,16,256]{2,0,1:T(8,128)(2,1)} %copy.48), calls=%async_computation | async-start | bytes 2097152 | tf_op jit(solution)/shard_map/all_to_all | solution.py:135
  148.9 36.5 %all-to-all-start.1 = ((bf16[128,16,256]{2,0,1:T(8,128)(2,1)}), bf16[128,16,256]{2,0,1:T(8,128)(2,1)S(1)}, u32[]{:S(2)}, u32[]{:S(2)}) async-start(bf16[128,16,256]{2,0,1:T(8,128)(2,1)} %copy.51), calls=%async_computation.1 | async-start | bytes 2097152 | tf_op jit(solution)/shard_map/all_to_all | solution.py:136
  185.3 16.9 %copy-start.4 = (bf16[128,16,256]{2,0,1:T(8,128)(2,1)}, bf16[128,16,256]{2,0,1:T(8,128)(2,1)S(1)}, u32[]{:S(2)}) copy-start(bf16[128,16,256]{2,0,1:T(8,128)(2,1)S(1)} %all-to-all-done.1) | copy-start | bytes 3145732
  185.3 55.7 %all-to-all-start.2 = ((bf16[128,16,256]{2,0,1:T(8,128)(2,1)}), bf16[128,16,256]{2,0,1:T(8,128)(2,1)}, u32[]{:S(2)}, u32[]{:S(2)}) async-start(bf16[128,16,256]{2,0,1:T(8,128)(2,1)} %copy.54), calls=%async_computation.2 | async-start | bytes 2097152 | tf_op jit(solution)/shard_map/all_to_all | solution.py:138
  202.2 44.6 %copy-start.9 = (s32[1,16]{1,0:T(1,128)S(1)}, s32[1,16]{1,0:T(1,128)}, u32[]{:S(2)}) copy-start(s32[1,16]{1,0:T(1,128)} %param.15) | copy-start | bytes 196
  241.1 44.9 %all-to-all-start.3 = ((bf16[128,16,256]{2,0,1:T(8,128)(2,1)}), bf16[128,16,256]{2,0,1:T(8,128)(2,1)}, u32[]{:S(2)}, u32[]{:S(2)}) async-start(bf16[128,16,256]{2,0,1:T(8,128)(2,1)} %copy.57), calls=%async_computation.3 | async-start | bytes 2097152 | tf_op jit(solution)/shard_map/all_to_all | solution.py:137
  292.4 3.6 copy-start.3
  392.5 38.4 %all-to-all-start.5 = ((bf16[16,128,256]{2,1,0:T(8,128)(2,1)}), bf16[16,128,256]{2,1,0:T(8,128)(2,1)}, u32[]{:S(2)}, u32[]{:S(2)}) async-start(bf16[16,128,256]{2,1,0:T(8,128)(2,1)} %get-tuple-element.78), calls=%async_computation.5 | async-start | bytes 2097152 | tf_op jit(solution)/shard_map/all_to_all | solution.py:161
  396.8 223.2 %reduce-scatter.5.cloned.1.call-start = ((), (), s32[]{:S(2)}) async-start(), calls=%async_computation.7 | async-start | bytes 2228224
  440.5 2.1 copy-start.5
  440.5 2.2 copy-start.6
  442.8 1.8 copy-start.1
Sparse Core Ops, SparseCore 0:
  448.8 171.0 reduce-scatter.4
where the time goes:
time: 745 us; the launch traced here: 743 us
  waiting for transfers between devices  322 us (43%)
  blocking collectives  239 us (32%)
  local copies, waits for them, and re-layouts  63.5 us (9%)
  starting transfers between devices  45.8 us (6%)
  other arithmetic  32.8 us (4%)
  matrix products  22.9 us (3%)
  between operations  16.9 us (2%)
    unnamed x2, waiting for transfers between devices  169 us
    unnamed x1, blocking collectives  115 us
    all_gather x1, blocking collectives, on_device(): lax.all_gather(gain_k, 'seq', axis=0, tiled=True)  47.2 us
    all_to_all x1, blocking collectives, on_device(): lax.all_to_all(by_device(dquery.reshape(group_rows, local_width)), 'seq',...  43.8 us
    all_to_all x1, waiting for transfers between devices, on_device(): lax.all_to_all(cotangent, 'seq', split_axis=1, concat_axis=0, tiled=True)  36.6 us
    all_gather x1, blocking collectives, on_device(): lax.all_gather(gain_q, 'seq', axis=0, tiled=True)  33.7 us
    all_to_all x1, waiting for transfers between devices, on_device(): lax.all_to_all(v_in, 'seq', split_axis=1, concat_axis=0, tiled=True)  33.7 us
    all_to_all x1, waiting for transfers between devices, on_device(): lax.all_to_all(by_device(dkey_rows.reshape(group_rows, local_width)), 'se...  30.6 us
  transfers between devices with their start and end apart: 6, of which 6 were waited for; matrix products, arithmetic and copies ran while one was open for 3% of the time, Pallas kernels for 0%

commit v1 on v0

v1 whole, which is shorter than its diff:
```python
import functools

import jax
import jax.numpy as jnp
import numpy as np
from jax import lax
from jax.experimental import pallas as pl
from jax.experimental.pallas import tpu as pltpu
from jax.sharding import PartitionSpec as P

HEAD_DIM = 128
HALF = HEAD_DIM // 2
SPAN = 128
N_SEQ = 16
N_DP = 32
SPANS_CLIP = 8
CLIP = SPAN * SPANS_CLIP
LOCAL_HEADS = 2
WIDTH = LOCAL_HEADS * HEAD_DIM
HD_ALL = 4096
EPSILON = 1e-06
MESH = pl.DeviceIdType.MESH
FACTOR = HEAD_DIM ** (-0.5)
LOG2E = 1.4426950408889634


def rope_constants():
    frequency = 10000.0 ** (-np.arange(HALF, dtype=np.float64) / HALF)
    angles = frequency[None, :, None] * np.arange(CLIP, dtype=np.float64).reshape(SPANS_CLIP, 1, SPAN)
    return np.cos(angles).astype(np.float32), np.sin(angles).astype(np.float32)


def kernel(
    owner, cos_hbm, sin_hbm, gq_hbm, gk_hbm, q_hbm, k_hbm, v_hbm, c_hbm,
    outq, outk,
    qb, kb, vb, cb, own_rows, stat_out, stat, cosr, sinr, gain_rows, gq, gk,
    krot, kcs, vord, qhat, qrot, probs, acc, red, holder,
    ssem, rsem, stat_ssem, stat_rsem, red_ssem, red_rsem, own_sem, misc_sem,
):
    dp = lax.axis_index("dp")
    me = lax.axis_index("seq")
    x, zh, core = me // 4, (me // 2) % 2, me % 2
    hbm = (q_hbm, k_hbm, v_hbm, c_hbm)
    bufs = (qb, kb, vb, cb)
    Q, K, V, C = range(4)

    def to(k):
        far, dx, dc = k // 8, (k // 2) % 4, k % 2
        return ((x + dx) % 4) * 4 + ((zh + far) % 2) * 2 + (core + dc) % 2

    def source(k):
        far, dx, dc = k // 8, (k // 2) % 4, k % 2
        return ((x + 4 - dx) % 4) * 4 + ((zh + far) % 2) * 2 + (core + dc) % 2

    def send(a, k):
        t = to(k)
        return pltpu.make_async_remote_copy(
            src_ref=hbm[a].at[:, pl.ds(pl.multiple_of(t * WIDTH, WIDTH), WIDTH)],
            dst_ref=bufs[a].at[me],
            send_sem=ssem.at[a, k],
            recv_sem=rsem.at[a, k],
            device_id=(dp, t),
            device_id_type=MESH,
        )

    def arrival(a, k):
        j = source(k)
        return pltpu.make_async_remote_copy(
            src_ref=bufs[a].at[j],
            dst_ref=bufs[a].at[j],
            send_sem=ssem.at[a, k],
            recv_sem=rsem.at[a, k],
            device_id=(dp, j),
            device_id_type=MESH,
        )

    def own_copy(a):
        return pltpu.make_async_copy(
            hbm[a].at[:, pl.ds(pl.multiple_of(me * WIDTH, WIDTH), WIDTH)], bufs[a].at[me], own_sem.at[a]
        )

    def send_stat(k):
        t = to(k)
        return pltpu.make_async_remote_copy(
            src_ref=stat_out,
            dst_ref=stat.at[me],
            send_sem=stat_ssem.at[k],
            recv_sem=stat_rsem.at[k],
            device_id=(dp, t),
            device_id_type=MESH,
        )

    def arrival_stat(k):
        j = source(k)
        return pltpu.make_async_remote_copy(
            src_ref=stat.at[j],
            dst_ref=stat.at[j],
            send_sem=stat_ssem.at[k],
            recv_sem=stat_rsem.at[k],
            device_id=(dp, j),
            device_id_type=MESH,
        )

    def send_acc(i):
        t = (dp + i) % N_DP
        return pltpu.make_async_remote_copy(
            src_ref=acc.at[t],
            dst_ref=red.at[dp],
            send_sem=red_ssem.at[i],
            recv_sem=red_rsem.at[i],
            device_id=(t, me),
            device_id_type=MESH,
        )

    def arrival_acc(i):
        j = (dp + N_DP - i) % N_DP
        return pltpu.make_async_remote_copy(
            src_ref=red.at[j],
            dst_ref=red.at[j],
            send_sem=red_ssem.at[i],
            recv_sem=red_rsem.at[i],
            device_id=(j, me),
            device_id_type=MESH,
        )

    def loop(lo, hi, body):
        def step(i, carry):
            body(i)
            return carry

        lax.fori_loop(lo, hi, step, 0)

    barrier = pltpu.get_barrier_semaphore()
    loop(1, N_SEQ, lambda k: pl.semaphore_signal(barrier, inc=1, device_id=(dp, to(k)), device_id_type=MESH))
    loop(
        1, N_DP,
        lambda i: pl.semaphore_signal(barrier, inc=1, device_id=((dp + i) % N_DP, me), device_id_type=MESH),
    )
    misc = [
        pltpu.make_async_copy(q_hbm, own_rows.at[0], misc_sem.at[0]),
        pltpu.make_async_copy(k_hbm, own_rows.at[1], misc_sem.at[1]),
        pltpu.make_async_copy(cos_hbm, cosr, misc_sem.at[2]),
        pltpu.make_async_copy(sin_hbm, sinr, misc_sem.at[3]),
        pltpu.make_async_copy(gq_hbm, gain_rows.at[0], misc_sem.at[4]),
        pltpu.make_async_copy(gk_hbm, gain_rows.at[1], misc_sem.at[5]),
    ]
    for copy in misc:
        copy.start()
    pl.semaphore_wait(barrier, N_SEQ - 1 + N_DP - 1)

    loop(8, 16, lambda k: send(K, k).start())
    for a in range(4):
        own_copy(a).start()

    for i in range(2):
        misc[i].wait()

        def add(b, total):
            block = own_rows[i, :, pl.ds(pl.multiple_of(b * HEAD_DIM, HEAD_DIM), HEAD_DIM)].astype(jnp.float32)
            return total + block * block

        total = lax.fori_loop(0, HD_ALL // HEAD_DIM, add, jnp.zeros((SPAN, HEAD_DIM), jnp.float32))
        mean = jnp.sum(total.T, axis=0, keepdims=True) * (1.0 / HD_ALL)
        stat_out[i : i + 1, :] = 1.0 / jnp.sqrt(mean + EPSILON)
    stat_out[2:8, :] = jnp.zeros((6, SPAN), jnp.float32)
    loop(1, N_SEQ, lambda k: send_stat(k).start())
    stat[pl.ds(me, 1)] = stat_out[...].reshape(1, 8, SPAN)

    loop(8, 16, lambda k: send(Q, k).start())
    loop(1, 8, lambda k: send(K, k).start())
    loop(1, 8, lambda k: send(Q, k).start())
    loop(8, 16, lambda k: send(V, k).start())
    loop(1, 8, lambda k: send(V, k).start())
    loop(1, 8, lambda k: send(C, k).start())
    loop(8, 16, lambda k: send(C, k).start())

    for s in range(N_SEQ):
        place = jnp.int32(0)
        for j in range(N_SEQ):
            place = jnp.maximum(place, jnp.where(owner[0, j] == s, jnp.int32(j), jnp.int32(0)))
        holder[s] = place
    for copy in misc[2:]:
        copy.wait()
    for h in range(LOCAL_HEADS):
        gq[h] = jnp.broadcast_to(gain_rows[0, h : h + 1, :], (SPAN, HEAD_DIM)).T
        gk[h] = jnp.broadcast_to(gain_rows[1, h : h + 1, :], (SPAN, HEAD_DIM)).T
    acc[...] = jnp.zeros(acc.shape, jnp.float32)
    for a in range(4):
        own_copy(a).wait()

    def wait_key(k):
        arrival_stat(k).wait_recv()
        arrival(K, k).wait_recv()

    loop(1, N_SEQ, wait_key)

    def key_span(s):
        j = holder[s]
        clip, p = s // SPANS_CLIP, s % SPANS_CLIP
        cols = pl.ds(pl.multiple_of(p * SPAN, SPAN), SPAN)
        cs, sn = cosr[p], sinr[p]
        scale = stat[j][1:2, :]
        raw = kb[j]
        for h in range(LOCAL_HEADS):
            hat = raw[:, h * HEAD_DIM : (h + 1) * HEAD_DIM].astype(jnp.float32).T * scale
            lo, hi = hat[:HALF], hat[HALF:]
            lc, hc, ls, hs = lo * cs, hi * cs, lo * sn, hi * sn
            gain = gk[h]
            gl, gh = gain[:HALF], gain[HALF:]
            kcs[h, clip, 0:HALF, cols] = lc.astype(jnp.bfloat16)
            kcs[h, clip, HALF : 2 * HALF, cols] = hc.astype(jnp.bfloat16)
            kcs[h, clip, 2 * HALF : 3 * HALF, cols] = ls.astype(jnp.bfloat16)
            kcs[h, clip, 3 * HALF : 4 * HALF, cols] = hs.astype(jnp.bfloat16)
            rot = jnp.concatenate([gl * lc - gh * hs, gl * ls + gh * hc], axis=0)
            krot[h, clip, cols, :] = rot.T.astype(jnp.bfloat16)

    loop(0, N_SEQ, key_span)

    def query_span(k):
        @pl.when(k > 0)
        def _():
            arrival(Q, k).wait_recv()

        j = source(k)
        slot = owner[0, j]
        clip, p = lax.shift_right_logical(slot, 3), lax.bitwise_and(slot, 7)
        cs, sn = cosr[p], sinr[p]
        scale = stat[j][0:1, :]
        raw = qb[j]
        for h in range(LOCAL_HEADS):
            hat = raw[:, h * HEAD_DIM : (h + 1) * HEAD_DIM].astype(jnp.float32).T * scale
            qhat[k, h] = hat
            scaled = hat * gq[h]
            lo, hi = scaled[:HALF], scaled[HALF:]
            rot = jnp.concatenate([lo * cs - hi * sn, lo * sn + hi * cs], axis=0).astype(jnp.bfloat16)
            qrot[k, h] = rot
            scores = jnp.dot(krot[h, clip], rot, preferred_element_type=jnp.float32)
            peak = jnp.max(scores, axis=0, keepdims=True)
            lifted = jnp.exp2((scores - peak) * (FACTOR * LOG2E))
            probs[k, h] = lifted * (1.0 / jnp.sum(lifted, axis=0, keepdims=True))

    loop(0, N_SEQ, query_span)

    loop(1, N_SEQ, lambda k: arrival(V, k).wait_recv())

    def value_span(s):
        raw = vb[holder[s]]
        rows = pl.ds(pl.multiple_of((s % SPANS_CLIP) * SPAN, SPAN), SPAN)
        for h in range(LOCAL_HEADS):
            vord[h, s // SPANS_CLIP, rows, :] = raw[:, h * HEAD_DIM : (h + 1) * HEAD_DIM]

    loop(0, N_SEQ, value_span)

    def grad_span(k):
        @pl.when(k > 0)
        def _():
            arrival(C, k).wait_recv()

        j = source(k)
        slot = owner[0, j]
        clip, p = lax.shift_right_logical(slot, 3), lax.bitwise_and(slot, 7)
        cs, sn = cosr[p], sinr[p]
        raw = cb[j]
        for h in range(LOCAL_HEADS):
            slopes = lax.dot_general(
                vord[h, clip], raw[:, h * HEAD_DIM : (h + 1) * HEAD_DIM],
                (((1,), (1,)), ((), ())), preferred_element_type=jnp.float32,
            )
            weights = probs[k, h]
            center = jnp.sum(weights * slopes, axis=0, keepdims=True)
            dscore = (weights * (slopes - center)).astype(jnp.bfloat16)
            both = jnp.dot(kcs[h, clip], dscore, preferred_element_type=jnp.float32) * FACTOR
            ul, uh, wl, wh = (both[i * HALF : (i + 1) * HALF] for i in range(4))
            gain = gk[h]
            gl, gh = gain[:HALF], gain[HALF:]
            dl, dh = gl * ul - gh * wh, gl * wl + gh * uh
            hat = qhat[k, h]
            rot = qrot[k, h].astype(jnp.float32)
            ql, qh = rot[:HALF], rot[HALF:]
            gradq = jnp.concatenate([(dl * cs + dh * sn) * hat[:HALF], (dh * cs - dl * sn) * hat[HALF:]], axis=0)
            gradk = jnp.concatenate([ql * ul + qh * wl, qh * uh - ql * wh], axis=0)
            rows = slice(h * 16, (h + 1) * 16)
            acc[rows, 0] += gradq.reshape(16, 8, SPAN)
            acc[rows, 1] += gradk.reshape(16, 8, SPAN)

    loop(0, N_SEQ, grad_span)

    loop(1, N_DP, lambda i: send_acc(i).start())
    red[pl.ds(dp, 1)] = acc[pl.ds(dp, 1)]
    loop(1, N_DP, lambda i: arrival_acc(i).wait_recv())
    total = jnp.sum(red[...], axis=0)
    outq[...] = jnp.sum(total[0].T, axis=0, keepdims=True)
    outk[...] = jnp.sum(total[1].T, axis=0, keepdims=True)

    def wait_sends(k):
        send_stat(k).wait_send()
        for a in range(4):
            send(a, k).wait_send()

    loop(1, N_SEQ, wait_sends)
    loop(1, N_DP, lambda i: send_acc(i).wait_send())


def on_device(cos, sin, q_in, k_in, v_in, cotangent, owner, gain_q, gain_k):
    bf16, f32, dma = jnp.bfloat16, jnp.float32, pltpu.SemaphoreType.DMA
    anywhere = pl.BlockSpec(memory_space=pl.ANY)
    in_vmem = pl.BlockSpec(memory_space=pltpu.VMEM)
    span_buf = pltpu.VMEM((N_SEQ, SPAN, WIDTH), bf16)
    outq, outk = pl.pallas_call(
        kernel,
        out_shape=[jax.ShapeDtypeStruct((1, 8), f32)] * 2,
        in_specs=[pl.BlockSpec(memory_space=pltpu.SMEM)] + [anywhere] * 8,
        out_specs=[in_vmem] * 2,
        scratch_shapes=[
            span_buf, span_buf, span_buf, span_buf,
            pltpu.VMEM((2, SPAN, HD_ALL), bf16),
            pltpu.VMEM((8, SPAN), f32),
            pltpu.VMEM((N_SEQ, 8, SPAN), f32),
            pltpu.VMEM((SPANS_CLIP, HALF, SPAN), f32),
            pltpu.VMEM((SPANS_CLIP, HALF, SPAN), f32),
            pltpu.VMEM((2, LOCAL_HEADS, HEAD_DIM), f32),
            pltpu.VMEM((LOCAL_HEADS, HEAD_DIM, SPAN), f32),
            pltpu.VMEM((LOCAL_HEADS, HEAD_DIM, SPAN), f32),
            pltpu.VMEM((LOCAL_HEADS, 2, CLIP, HEAD_DIM), bf16),
            pltpu.VMEM((LOCAL_HEADS, 2, 2 * HEAD_DIM, CLIP), bf16),
            pltpu.VMEM((LOCAL_HEADS, 2, CLIP, HEAD_DIM), bf16),
            pltpu.VMEM((N_SEQ, LOCAL_HEADS, HEAD_DIM, SPAN), f32),
            pltpu.VMEM((N_SEQ, LOCAL_HEADS, HEAD_DIM, SPAN), bf16),
            pltpu.VMEM((N_SEQ, LOCAL_HEADS, CLIP, SPAN), f32),
            pltpu.VMEM((N_DP, 2, 8, SPAN), f32),
            pltpu.VMEM((N_DP, 2, 8, SPAN), f32),
            pltpu.SMEM((N_SEQ,), jnp.int32),
            dma((4, N_SEQ)), dma((4, N_SEQ)),
            dma((N_SEQ,)), dma((N_SEQ,)),
            dma((N_DP,)), dma((N_DP,)),
            dma((4,)), dma((6,)),
        ],
        compiler_params=pltpu.CompilerParams(
            collective_id=0, has_side_effects=True, vmem_limit_bytes=56 * 2**20
        ),
    )(
        owner, cos, sin, gain_q.reshape(LOCAL_HEADS, HEAD_DIM), gain_k.reshape(LOCAL_HEADS, HEAD_DIM),
        q_in, k_in, v_in, cotangent,
    )
    return outq.reshape(8), outk.reshape(8)


def solution(mesh):
    cos, sin = rope_constants()
    mapped = jax.shard_map(
        on_device,
        mesh=mesh,
        in_specs=(
            P(), P(),
            P(("dp", "seq"), None),
            P(("dp", "seq"), None),
            P(("dp", "seq"), None),
            P(("dp", "seq"), None),
            P("dp", None),
            P("seq"),
            P("seq"),
        ),
        out_specs=(P(("seq", "dp")), P(("seq", "dp"))),
        check_vma=False,
    )
    return lambda *args: mapped(jnp.asarray(cos), jnp.asarray(sin), *args)
```

time: 745 us -> 234 us (0.31)
  the two profiles are of different devices: /device:TPU:2 before, /device:TPU:1 now
where the time goes in v1:
time: 234 us; the launch traced here: 232 us
  Pallas kernels  229 us (98%)
    pallas_call x1, Pallas kernels, on_device(): pl.pallas_call(kernel, out_shape=[jax.ShapeDtypeStruct((1, 8), f32)] * 2,...  229 us

profile of v1, /device:TPU:1, one launch (start us, length us, event | category | flops | bytes accessed | tf_op | source)
XLA Modules:
  0.0 231.7 jit_solution(5519187007776138200)
XLA Ops:
  0.6 229.2 %shard_map.104 = (f32[1,8]{1,0:T(1,128)}, f32[1,8]{1,0:T(1,128)}) custom-call(s32[1,16]{1,0:T(1,128)} %owner.1, f32[8,64,128]{2,1,0:T(8,128)} %constant.4.clone.cos_hbm, f32[8,64,128]{2,1,0:T(8,128)} %constant.5.clone.sin_hbm, f32[2,128]{1,0:T(2,128)} %bitcast.4, f32[2,128]{1,0:T(2,128)} %bitcast.5, bf16[128,4096]{1,0:T(8,128)(2,1)} %q_hbm.1, ...), custom_call_target="tpu_custom_call" | custom-call | tf_op jit(solution)/shard_map/pallas_call | solution.py:309
  229.8 0.0 copy-start.1
  229.9 0.7 copy-done.1
  230.5 0.0 copy-start
  230.5 0.5 copy.13
  231.0 0.1 copy-done
  231.1 0.5 copy.14
Async XLA Ops:
  229.8 0.7 copy-start.1
  230.5 0.6 copy-start

commit v2 on v1

v2 whole, which is shorter than its diff:
```python
import functools

import jax
import jax.numpy as jnp
import numpy as np
from jax import lax
from jax.experimental import pallas as pl
from jax.experimental.pallas import tpu as pltpu
from jax.sharding import PartitionSpec as P

HEAD_DIM = 128
HALF = HEAD_DIM // 2
SPAN = 128
N_SEQ = 16
N_DP = 32
SPANS_CLIP = 8
CLIP = SPAN * SPANS_CLIP
LOCAL_HEADS = 2
WIDTH = LOCAL_HEADS * HEAD_DIM
HD_ALL = 4096
EPSILON = 1e-06
MESH = pl.DeviceIdType.MESH
FACTOR = HEAD_DIM ** (-0.5)
LOG2E = 1.4426950408889634
PARTS = [slice(i, i + 256) for i in range(0, CLIP, 256)]


def rope_constants():
    frequency = 10000.0 ** (-np.arange(HALF, dtype=np.float64) / HALF)
    angles = frequency[None, :, None] * np.arange(CLIP, dtype=np.float64).reshape(SPANS_CLIP, 1, SPAN)
    return np.cos(angles).astype(np.float32), np.sin(angles).astype(np.float32)


def kernel(
    owner_hbm, cos_hbm, sin_hbm, gq_hbm, gk_hbm, q_hbm, k_hbm, v_hbm, c_hbm,
    outq, outk,
    qb, kb, vb, cb, own_rows, stat_out, stat, cosr, sinr, gain_rows, gq, gk,
    krot, kcs, vord, qhat, qrot, probs, slopes, acc, sums, red, holder, held, owner,
    ssem, rsem, stat_ssem, stat_rsem, red_ssem, red_rsem, own_sem, misc_sem,
):
    dp = lax.axis_index("dp")
    me = lax.axis_index("seq")
    x, zh, core = me // 4, (me // 2) % 2, me % 2
    hbm = (q_hbm, k_hbm, v_hbm, c_hbm)
    bufs = (qb, kb, vb, cb)
    Q, K, V, C = range(4)

    ahead = [((x + d) % 4) * 4 for d in range(4)]
    halves = [zh * 2, (1 - zh) * 2]
    cores = [core, 1 - core]

    def offset(k):
        return k // 8, (0, 2, 1, 3)[k % 4], (k // 4) % 2

    def to(k):
        far, dx, dc = offset(k)
        return ahead[dx] + halves[far] + cores[dc]

    def source(k):
        far, dx, dc = offset(k)
        return ahead[(4 - dx) % 4] + halves[far] + cores[dc]

    def send(a, k):
        t = to(k)
        return pltpu.make_async_remote_copy(
            src_ref=hbm[a].at[:, pl.ds(pl.multiple_of(t * WIDTH, WIDTH), WIDTH)],
            dst_ref=bufs[a].at[k],
            send_sem=ssem.at[a, k],
            recv_sem=rsem.at[a, k],
            device_id=(dp, t),
            device_id_type=MESH,
        )

    def arrival(a, k):
        return pltpu.make_async_remote_copy(
            src_ref=bufs[a].at[k],
            dst_ref=bufs[a].at[k],
            send_sem=ssem.at[a, k],
            recv_sem=rsem.at[a, k],
            device_id=(dp, me),
            device_id_type=MESH,
        )

    def own_copy(a):
        return pltpu.make_async_copy(
            hbm[a].at[:, pl.ds(pl.multiple_of(me * WIDTH, WIDTH), WIDTH)], bufs[a].at[0], own_sem.at[a]
        )

    def send_stat(k):
        return pltpu.make_async_remote_copy(
            src_ref=stat_out,
            dst_ref=stat.at[k],
            send_sem=stat_ssem.at[k],
            recv_sem=stat_rsem.at[k],
            device_id=(dp, to(k)),
            device_id_type=MESH,
        )

    def arrival_stat(k):
        return pltpu.make_async_remote_copy(
            src_ref=stat.at[k],
            dst_ref=stat.at[k],
            send_sem=stat_ssem.at[k],
            recv_sem=stat_rsem.at[k],
            device_id=(dp, me),
            device_id_type=MESH,
        )

    y, z = dp // 8, dp % 8
    ybits, zbits = ((y // 2) % 2, y % 2), ((z // 4) % 2, (z // 2) % 2, z % 2)

    def flipped(bits, mask):
        total = jnp.int32(0)
        for n, bit in enumerate(bits):
            place = 1 << (len(bits) - 1 - n)
            total = total + ((1 - bit) if mask & place else bit) * place
        return total

    rows_y = [flipped(ybits, m) for m in range(4)]
    parts_z = [flipped(zbits, m) for m in range(8)]

    def partner(i):
        m = 31 - i
        return rows_y[m % 4] * 8 + parts_z[m // 4]

    def send_acc(i):
        return pltpu.make_async_remote_copy(
            src_ref=sums.at[rows_y[(31 - i) % 4]],
            dst_ref=red.at[i],
            send_sem=red_ssem.at[i],
            recv_sem=red_rsem.at[i],
            device_id=(partner(i), me),
            device_id_type=MESH,
        )

    def arrival_acc(i):
        return pltpu.make_async_remote_copy(
            src_ref=red.at[i],
            dst_ref=red.at[i],
            send_sem=red_ssem.at[i],
            recv_sem=red_rsem.at[i],
            device_id=(dp, me),
            device_id_type=MESH,
        )

    def each(lo, hi, body):
        for i in range(lo, hi):
            body(i)

    def loop(lo, hi, body):
        def step(i, carry):
            body(i)
            return carry

        lax.fori_loop(lo, hi, step, 0)

    barrier = pltpu.get_barrier_semaphore()
    each(
        0, N_SEQ - 1,
        lambda i: pl.semaphore_signal(barrier, inc=1, device_id=(dp, to(15 - i)), device_id_type=MESH),
    )
    each(
        0, N_DP - 1,
        lambda i: pl.semaphore_signal(barrier, inc=1, device_id=(partner(i), me), device_id_type=MESH),
    )
    misc = [
        pltpu.make_async_copy(q_hbm, own_rows.at[0], misc_sem.at[0]),
        pltpu.make_async_copy(k_hbm, own_rows.at[1], misc_sem.at[1]),
        pltpu.make_async_copy(cos_hbm, cosr, misc_sem.at[2]),
        pltpu.make_async_copy(sin_hbm, sinr, misc_sem.at[3]),
        pltpu.make_async_copy(gq_hbm, gain_rows.at[0], misc_sem.at[4]),
        pltpu.make_async_copy(gk_hbm, gain_rows.at[1], misc_sem.at[5]),
        pltpu.make_async_copy(owner_hbm, owner, misc_sem.at[6]),
    ]
    for copy in misc:
        copy.start()
    pl.semaphore_wait(barrier, N_SEQ - 1 + N_DP - 1)

    each(8, 16, lambda k: send(K, k).start())
    for a in range(4):
        own_copy(a).start()

    for i in range(2):
        misc[i].wait()

        def add(b, total):
            block = own_rows[i, :, pl.ds(pl.multiple_of(b * HEAD_DIM, HEAD_DIM), HEAD_DIM)].astype(jnp.float32)
            return total + block * block

        total = lax.fori_loop(0, HD_ALL // HEAD_DIM, add, jnp.zeros((SPAN, HEAD_DIM), jnp.float32))
        mean = jnp.sum(total.T, axis=0, keepdims=True) * (1.0 / HD_ALL)
        stat_out[i : i + 1, :] = 1.0 / jnp.sqrt(mean + EPSILON)
    stat_out[2:8, :] = jnp.zeros((6, SPAN), jnp.float32)
    each(1, N_SEQ, lambda k: send_stat(k).start())
    stat[0:1] = stat_out[...].reshape(1, 8, SPAN)

    each(8, 16, lambda k: send(Q, k).start())
    for a in range(4):
        each(1, 8, lambda k: send(a, k).start())
    each(8, 16, lambda k: send(V, k).start())
    each(8, 16, lambda k: send(C, k).start())

    for copy in misc[2:]:
        copy.wait()

    for k in range(N_SEQ):
        held[k] = owner[0, source(k)]

    def find(s):
        place = jnp.int32(0)
        for k in range(N_SEQ):
            place = jnp.maximum(place, jnp.where(held[k] == s, jnp.int32(k), jnp.int32(0)))
        holder[s] = place

    loop(0, N_SEQ, find)
    for h in range(LOCAL_HEADS):
        gq[h] = jnp.broadcast_to(gain_rows[0, h : h + 1, :], (SPAN, HEAD_DIM)).T
        gk[h] = jnp.broadcast_to(gain_rows[1, h : h + 1, :], (SPAN, HEAD_DIM)).T
    acc[...] = jnp.zeros(acc.shape, jnp.float32)
    for a in range(4):
        own_copy(a).wait()

    def wait_key(k):
        arrival_stat(k).wait_recv()
        arrival(K, k).wait_recv()

    each(1, N_SEQ, wait_key)

    def key_span(s):
        j = holder[s]
        clip, p = s // SPANS_CLIP, s % SPANS_CLIP
        cols = pl.ds(pl.multiple_of(p * SPAN, SPAN), SPAN)
        cs, sn = cosr[p], sinr[p]
        scale = stat[j][1:2, :]
        raw = kb[j]
        for h in range(LOCAL_HEADS):
            hat = raw[:, h * HEAD_DIM : (h + 1) * HEAD_DIM].astype(jnp.float32).T * scale
            lo, hi = hat[:HALF], hat[HALF:]
            lc, hc, ls, hs = lo * cs, hi * cs, lo * sn, hi * sn
            gain = gk[h]
            gl, gh = gain[:HALF], gain[HALF:]
            kcs[h, clip, 0:HALF, cols] = lc.astype(jnp.bfloat16)
            kcs[h, clip, HALF : 2 * HALF, cols] = hc.astype(jnp.bfloat16)
            kcs[h, clip, 2 * HALF : 3 * HALF, cols] = ls.astype(jnp.bfloat16)
            kcs[h, clip, 3 * HALF : 4 * HALF, cols] = hs.astype(jnp.bfloat16)
            rot = jnp.concatenate([gl * lc - gh * hs, gl * ls + gh * hc], axis=0)
            krot[h, clip, cols, :] = rot.T.astype(jnp.bfloat16)

    loop(0, N_SEQ, key_span)

    def query_span(k):
        @pl.when(k > 0)
        def _():
            arrival(Q, k).wait_recv()

        slot = held[k]
        clip, p = lax.shift_right_logical(slot, 3), lax.bitwise_and(slot, 7)
        cs, sn = cosr[p], sinr[p]
        scale = stat[k][0:1, :]
        raw = qb[k]
        for h in range(LOCAL_HEADS):
            hat = raw[:, h * HEAD_DIM : (h + 1) * HEAD_DIM].astype(jnp.float32).T * scale
            qhat[k, h] = hat
            scaled = hat * gq[h]
            lo, hi = scaled[:HALF], scaled[HALF:]
            rot = jnp.concatenate([lo * cs - hi * sn, lo * sn + hi * cs], axis=0).astype(jnp.bfloat16)
            qrot[k, h] = rot
            scores = jnp.dot(krot[h, clip], rot, preferred_element_type=jnp.float32)
            peak = jnp.max(scores, axis=0, keepdims=True)
            lifted = jnp.exp2((scores - peak) * (FACTOR * LOG2E))
            probs[k, h] = lifted * (1.0 / jnp.sum(lifted, axis=0, keepdims=True))

    loop(0, N_SEQ, query_span)

    each(1, N_SEQ, lambda k: arrival(V, k).wait_recv())

    def value_span(s):
        raw = vb[holder[s]]
        rows = pl.ds(pl.multiple_of((s % SPANS_CLIP) * SPAN, SPAN), SPAN)
        for h in range(LOCAL_HEADS):
            vord[h, s // SPANS_CLIP, rows, :] = raw[:, h * HEAD_DIM : (h + 1) * HEAD_DIM]

    loop(0, N_SEQ, value_span)

    def grad_span(k):
        @pl.when(k > 0)
        def _():
            arrival(C, k).wait_recv()

        slot = held[k]
        clip, p = lax.shift_right_logical(slot, 3), lax.bitwise_and(slot, 7)
        cs, sn = cosr[p], sinr[p]
        raw = cb[k]
        for h in range(LOCAL_HEADS):
            cotangent = raw[:, h * HEAD_DIM : (h + 1) * HEAD_DIM]
            total = None
            for part in PARTS:
                slopes[h, part] = lax.dot_general(
                    vord[h, clip, part, :], cotangent, (((1,), (1,)), ((), ())), preferred_element_type=jnp.float32
                )
                share = jnp.sum((probs[k, h, part] * slopes[h, part]).reshape(-1, 8, SPAN), axis=0)
                total = share if total is None else total + share
            center = jnp.sum(total, axis=0, keepdims=True)
            both = None
            for part in PARTS:
                dscore = (probs[k, h, part] * (slopes[h, part] - center)).astype(jnp.bfloat16)
                share = jnp.dot(kcs[h, clip, :, part], dscore, preferred_element_type=jnp.float32)
                both = share if both is None else both + share
            both = both * FACTOR
            ul, uh, wl, wh = (both[i * HALF : (i + 1) * HALF] for i in range(4))
            gain = gk[h]
            gl, gh = gain[:HALF], gain[HALF:]
            dl, dh = gl * ul - gh * wh, gl * wl + gh * uh
            hat = qhat[k, h]
            rot = qrot[k, h].astype(jnp.float32)
            ql, qh = rot[:HALF], rot[HALF:]
            acc[2 * h, :HALF] += (dl * cs + dh * sn) * hat[:HALF]
            acc[2 * h, HALF:] += ql * ul + qh * wl
            acc[2 * h + 1, :HALF] += (dh * cs - dl * sn) * hat[HALF:]
            acc[2 * h + 1, HALF:] += qh * uh - ql * wh

    loop(0, N_SEQ, grad_span)

    for i in range(4):
        sums[i] = jnp.sum(acc[i].T, axis=0, keepdims=True)
    each(0, N_DP - 1, lambda i: send_acc(i).start())
    red[N_DP - 1 : N_DP] = sums[pl.ds(y, 1)]

    def wait_sends(k):
        send_stat(k).wait_send()
        for a in range(4):
            send(a, k).wait_send()

    each(1, N_SEQ, wait_sends)
    each(0, N_DP - 1, lambda i: send_acc(i).wait_send())
    each(0, N_DP - 1, lambda i: arrival_acc(i).wait_recv())
    total = jnp.broadcast_to(jnp.sum(red[...], axis=0), (8, SPAN))
    mine = pltpu.roll(total, (SPAN - 8 * z) % SPAN, 1)
    outq[...] = mine[0, 0:8]
    outk[...] = mine[0, HALF : HALF + 8]


def on_device(cos, sin, q_in, k_in, v_in, cotangent, owner, gain_q, gain_k):
    bf16, f32, dma = jnp.bfloat16, jnp.float32, pltpu.SemaphoreType.DMA
    anywhere = pl.BlockSpec(memory_space=pl.ANY)
    in_vmem = pl.BlockSpec(memory_space=pltpu.VMEM)
    span_buf = pltpu.VMEM((N_SEQ, SPAN, WIDTH), bf16)
    outq, outk = pl.pallas_call(
        kernel,
        out_shape=[jax.ShapeDtypeStruct((8,), f32)] * 2,
        in_specs=[anywhere] * 9,
        out_specs=[in_vmem] * 2,
        scratch_shapes=[
            span_buf, span_buf, span_buf, span_buf,
            pltpu.VMEM((2, SPAN, HD_ALL), bf16),
            pltpu.VMEM((8, SPAN), f32),
            pltpu.VMEM((N_SEQ, 8, SPAN), f32),
            pltpu.VMEM((SPANS_CLIP, HALF, SPAN), f32),
            pltpu.VMEM((SPANS_CLIP, HALF, SPAN), f32),
            pltpu.VMEM((2, LOCAL_HEADS, HEAD_DIM), f32),
            pltpu.VMEM((LOCAL_HEADS, HEAD_DIM, SPAN), f32),
            pltpu.VMEM((LOCAL_HEADS, HEAD_DIM, SPAN), f32),
            pltpu.VMEM((LOCAL_HEADS, 2, CLIP, HEAD_DIM), bf16),
            pltpu.VMEM((LOCAL_HEADS, 2, 2 * HEAD_DIM, CLIP), bf16),
            pltpu.VMEM((LOCAL_HEADS, 2, CLIP, HEAD_DIM), bf16),
            pltpu.VMEM((N_SEQ, LOCAL_HEADS, HEAD_DIM, SPAN), f32),
            pltpu.VMEM((N_SEQ, LOCAL_HEADS, HEAD_DIM, SPAN), bf16),
            pltpu.VMEM((N_SEQ, LOCAL_HEADS, CLIP, SPAN), f32),
            pltpu.VMEM((LOCAL_HEADS, CLIP, SPAN), f32),
            pltpu.VMEM((4, SPAN, SPAN), f32),
            pltpu.VMEM((4, 1, SPAN), f32),
            pltpu.VMEM((N_DP, 1, SPAN), f32),
            pltpu.SMEM((N_SEQ,), jnp.int32),
            pltpu.SMEM((N_SEQ,), jnp.int32),
            pltpu.SMEM((1, N_SEQ), jnp.int32),
            dma((4, N_SEQ)), dma((4, N_SEQ)),
            dma((N_SEQ,)), dma((N_SEQ,)),
            dma((N_DP,)), dma((N_DP,)),
            dma((4,)), dma((7,)),
        ],
        compiler_params=pltpu.CompilerParams(
            collective_id=0, has_side_effects=True, vmem_limit_bytes=56 * 2**20
        ),
    )(
        owner, cos, sin, gain_q.reshape(LOCAL_HEADS, HEAD_DIM), gain_k.reshape(LOCAL_HEADS, HEAD_DIM),
        q_in, k_in, v_in, cotangent,
    )
    return outq, outk


def solution(mesh):
    cos, sin = rope_constants()
    mapped = jax.shard_map(
        on_device,
        mesh=mesh,
        in_specs=(
            P(), P(),
            P(("dp", "seq"), None),
            P(("dp", "seq"), None),
            P(("dp", "seq"), None),
            P(("dp", "seq"), None),
            P("dp", None),
            P("seq"),
            P("seq"),
        ),
        out_specs=(P(("seq", "dp")), P(("seq", "dp"))),
        check_vma=False,
    )
    return lambda *args: mapped(jnp.asarray(cos), jnp.asarray(sin), *args)
```

time: 234 us -> 223 us (0.953); the launches traced: 232 us -> 223 us
  Pallas kernels: 229 us -> 221 us
    pallas_call x1, Pallas kernels: 229 us -> 221 us  [on_device(): pl.pallas_call(kernel, out_shape=[jax.ShapeDtypeStruct((8,), f32)] * 2, i...]
where the time goes in v2:
time: 223 us
  Pallas kernels  221 us (99%)
    pallas_call x1, Pallas kernels, on_device(): pl.pallas_call(kernel, out_shape=[jax.ShapeDtypeStruct((8,), f32)] * 2, i...  221 us

profile of v2, /device:TPU:1, one launch (start us, length us, event | category | flops | bytes accessed | tf_op | source)
XLA Modules:
  0.0 223.3 jit_solution(15371292456899555991)
XLA Ops:
  0.6 220.9 %shard_map.104 = (f32[8]{0:T(128)}, f32[8]{0:T(128)}) custom-call(s32[1,16]{1,0:T(1,128)} %owner_hbm.1, f32[8,64,128]{2,1,0:T(8,128)} %constant.4.clone.cos_hbm, f32[8,64,128]{2,1,0:T(8,128)} %constant.5.clone.sin_hbm, f32[2,128]{1,0:T(2,128)} %bitcast.2, f32[2,128]{1,0:T(2,128)} %bitcast.3, bf16[128,4096]{1,0:T(8,128)(2,1)} %q_hbm.1, ...), custom_call_target="tpu_custom_call" | custom-call | tf_op jit(solution)/shard_map/pallas_call | solution.py:348
  221.5 0.0 copy-start.1
  221.5 0.7 copy-done.1
  222.2 0.0 copy-start
  222.2 0.5 copy.13
  222.7 0.1 copy-done
  222.8 0.5 copy.14
Async XLA Ops:
  221.5 0.7 copy-start.1
  222.2 0.6 copy-start

commit v3 on v2

--- a/solution.py
+++ b/solution.py
@@ -33,7 +33,7 @@
 
 def kernel(
     owner_hbm, cos_hbm, sin_hbm, gq_hbm, gk_hbm, q_hbm, k_hbm, v_hbm, c_hbm,
-    outq, outk,
+    out,
     qb, kb, vb, cb, own_rows, stat_out, stat, cosr, sinr, gain_rows, gq, gk,
     krot, kcs, vord, qhat, qrot, probs, slopes, acc, sums, red, holder, held, owner,
     ssem, rsem, stat_ssem, stat_rsem, red_ssem, red_rsem, own_sem, misc_sem,
@@ -190,14 +190,13 @@
         total = lax.fori_loop(0, HD_ALL // HEAD_DIM, add, jnp.zeros((SPAN, HEAD_DIM), jnp.float32))
         mean = jnp.sum(total.T, axis=0, keepdims=True) * (1.0 / HD_ALL)
         stat_out[i : i + 1, :] = 1.0 / jnp.sqrt(mean + EPSILON)
-    stat_out[2:8, :] = jnp.zeros((6, SPAN), jnp.float32)
     each(1, N_SEQ, lambda k: send_stat(k).start())
-    stat[0:1] = stat_out[...].reshape(1, 8, SPAN)
-
+    stat[0:1] = stat_out[...].reshape(1, 2, SPAN)
+
+    each(8, 16, lambda k: send(V, k).start())
     each(8, 16, lambda k: send(Q, k).start())
     for a in range(4):
         each(1, 8, lambda k: send(a, k).start())
-    each(8, 16, lambda k: send(V, k).start())
     each(8, 16, lambda k: send(C, k).start())
 
     for copy in misc[2:]:
@@ -249,10 +248,6 @@
     loop(0, N_SEQ, key_span)
 
     def query_span(k):
-        @pl.when(k > 0)
-        def _():
-            arrival(Q, k).wait_recv()
-
         slot = held[k]
         clip, p = lax.shift_right_logical(slot, 3), lax.bitwise_and(slot, 7)
         cs, sn = cosr[p], sinr[p]
@@ -270,7 +265,8 @@
             lifted = jnp.exp2((scores - peak) * (FACTOR * LOG2E))
             probs[k, h] = lifted * (1.0 / jnp.sum(lifted, axis=0, keepdims=True))
 
-    loop(0, N_SEQ, query_span)
+    each(1, 8, lambda k: arrival(Q, k).wait_recv())
+    loop(0, 8, query_span)
 
     each(1, N_SEQ, lambda k: arrival(V, k).wait_recv())
 
@@ -283,10 +279,6 @@
     loop(0, N_SEQ, value_span)
 
     def grad_span(k):
-        @pl.when(k > 0)
-        def _():
-            arrival(C, k).wait_recv()
-
         slot = held[k]
         clip, p = lax.shift_right_logical(slot, 3), lax.bitwise_and(slot, 7)
         cs, sn = cosr[p], sinr[p]
@@ -319,7 +311,20 @@
             acc[2 * h + 1, :HALF] += (dh * cs - dl * sn) * hat[HALF:]
             acc[2 * h + 1, HALF:] += qh * uh - ql * wh
 
-    loop(0, N_SEQ, grad_span)
+    each(1, 8, lambda k: arrival(C, k).wait_recv())
+    loop(0, 8, grad_span)
+
+    def far_query(k):
+        arrival(Q, k).wait_recv()
+        query_span(k)
+
+    loop(8, N_SEQ, far_query)
+
+    def far_grad(k):
+        arrival(C, k).wait_recv()
+        grad_span(k)
+
+    loop(8, N_SEQ, far_grad)
 
     for i in range(4):
         sums[i] = jnp.sum(acc[i].T, axis=0, keepdims=True)
@@ -336,8 +341,7 @@
     each(0, N_DP - 1, lambda i: arrival_acc(i).wait_recv())
     total = jnp.broadcast_to(jnp.sum(red[...], axis=0), (8, SPAN))
     mine = pltpu.roll(total, (SPAN - 8 * z) % SPAN, 1)
-    outq[...] = mine[0, 0:8]
-    outk[...] = mine[0, HALF : HALF + 8]
+    out[...] = mine[0:1]
 
 
 def on_device(cos, sin, q_in, k_in, v_in, cotangent, owner, gain_q, gain_k):
@@ -345,16 +349,16 @@
     anywhere = pl.BlockSpec(memory_space=pl.ANY)
     in_vmem = pl.BlockSpec(memory_space=pltpu.VMEM)
     span_buf = pltpu.VMEM((N_SEQ, SPAN, WIDTH), bf16)
-    outq, outk = pl.pallas_call(
+    out = pl.pallas_call(
         kernel,
-        out_shape=[jax.ShapeDtypeStruct((8,), f32)] * 2,
+        out_shape=jax.ShapeDtypeStruct((1, SPAN), f32),
         in_specs=[anywhere] * 9,
-        out_specs=[in_vmem] * 2,
+        out_specs=in_vmem,
         scratch_shapes=[
             span_buf, span_buf, span_buf, span_buf,
             pltpu.VMEM((2, SPAN, HD_ALL), bf16),
-            pltpu.VMEM((8, SPAN), f32),
-            pltpu.VMEM((N_SEQ, 8, SPAN), f32),
+            pltpu.VMEM((2, SPAN), f32),
+            pltpu.VMEM((N_SEQ, 2, SPAN), f32),
             pltpu.VMEM((SPANS_CLIP, HALF, SPAN), f32),
             pltpu.VMEM((SPANS_CLIP, HALF, SPAN), f32),
             pltpu.VMEM((2, LOCAL_HEADS, HEAD_DIM), f32),
@@ -385,7 +389,7 @@
         owner, cos, sin, gain_q.reshape(LOCAL_HEADS, HEAD_DIM), gain_k.reshape(LOCAL_HEADS, HEAD_DIM),
         q_in, k_in, v_in, cotangent,
     )
-    return outq, outk
+    return out[0, 0:8], out[0, HALF : HALF + 8]
 
 
 def solution(mesh):

time: 223 us -> 217 us (0.973)
  Pallas kernels: 221 us -> 215 us
    pallas_call x1, Pallas kernels: 221 us -> 215 us  [on_device(): pl.pallas_call(kernel, out_shape=jax.ShapeDtypeStruct((1, SPAN), f32), in...]
where the time goes in v3:
time: 217 us
  Pallas kernels  215 us (99%)
    pallas_call x1, Pallas kernels, on_device(): pl.pallas_call(kernel, out_shape=jax.ShapeDtypeStruct((1, SPAN), f32), in...  215 us

profile of v3, /device:TPU:1, one launch (start us, length us, event | category | flops | bytes accessed | tf_op | source)
XLA Modules:
  0.0 217.3 jit_solution(15822041067855839729)
XLA Ops:
  0.6 215.4 %shard_map.104 = f32[1,128]{1,0:T(1,128)} custom-call(s32[1,16]{1,0:T(1,128)} %owner_hbm.1, f32[8,64,128]{2,1,0:T(8,128)} %constant.4.clone.cos_hbm, f32[8,64,128]{2,1,0:T(8,128)} %constant.5.clone.sin_hbm, f32[2,128]{1,0:T(2,128)} %bitcast.6, f32[2,128]{1,0:T(2,128)} %bitcast.7, bf16[128,4096]{1,0:T(8,128)(2,1)} %q_hbm.1, bf16[128,4096]{1,0:T(8,128)(2,1)} %k_hbm.1, ...), custom_call_target="tpu_custom_call" | custom-call | tf_op jit(solution)/shard_map/pallas_call | solution.py:352
  216.1 1.3 slice_bitcast_fusion

commit v4 on v3

--- a/solution.py
+++ b/solution.py
@@ -50,7 +50,7 @@
     cores = [core, 1 - core]
 
     def offset(k):
-        return k // 8, (0, 2, 1, 3)[k % 4], (k // 4) % 2
+        return k // 8, (2, 3, 1, 0)[k % 4] if k >= 8 else (0, 2, 1, 3)[k % 4], (k // 4) % 2
 
     def to(k):
         far, dx, dc = offset(k)

time: 217 us -> 217 us (level)
  no operation moved by 1% of the time
where the time goes in v4:
time: 217 us
  Pallas kernels  215 us (99%)
    pallas_call x1, Pallas kernels, on_device(): pl.pallas_call(kernel, out_shape=jax.ShapeDtypeStruct((1, SPAN), f32), in...  215 us

profile of v4, /device:TPU:1, one launch (start us, length us, event | category | flops | bytes accessed | tf_op | source)
XLA Modules:
  0.0 216.6 jit_solution(17015110513166655758)
XLA Ops:
  0.6 214.7 %shard_map.104 = f32[1,128]{1,0:T(1,128)} custom-call(s32[1,16]{1,0:T(1,128)} %owner_hbm.1, f32[8,64,128]{2,1,0:T(8,128)} %constant.4.clone.cos_hbm, f32[8,64,128]{2,1,0:T(8,128)} %constant.5.clone.sin_hbm, f32[2,128]{1,0:T(2,128)} %bitcast.6, f32[2,128]{1,0:T(2,128)} %bitcast.7, bf16[128,4096]{1,0:T(8,128)(2,1)} %q_hbm.1, bf16[128,4096]{1,0:T(8,128)(2,1)} %k_hbm.1, ...), custom_call_target="tpu_custom_call" | custom-call | tf_op jit(solution)/shard_map/pallas_call | solution.py:352
  215.4 1.3 slice_bitcast_fusion
